TPU v7x, 512 devices: a whole 4x8x8 slice. The times are simulated.
512 devices in a mesh: slab: 64 (over x, z, core), filt: 8 (over y).
Axes of the slice: x: 4, y: 8, z: 8, core: 2. Of those that a mesh axis runs over, the one named last changes fastest.
Arguments:
- volume: bfloat16 [128, 128, 16, 256], P('slab', 'filt'), may hold values from -6 to 6
- weights: bfloat16 [3, 3, 3, 128, 256], replicated, may hold values from -0.109375 to 0.109375
- out_error: bfloat16 [64, 256, 8, 128], P('slab', 'filt'), may hold values from -6 to 6
Outputs:
- in_grad: bfloat16 [128, 128, 16, 256], P('slab', None, 'filt')
- weight_grad: float32 [3, 3, 3, 128, 256], P(None, None, None, None, 'filt')
All inputs are finite; a program needn't handle non-finite values.
Results may differ from a plain program's by a relative error of at most 0.0049.
Values may be sent and summed in bfloat16 or wider, within the bound.
No kernel may reach another device: no remote copies, remote signals or barrier semaphores. Data moves between devices by JAX's collectives and lax.ppermute only.
A program may use at most 64 MiB of HBM per device.

v0:
```python
import math
import jax
import jax.numpy as jnp
from jax import lax
from jax.sharding import PartitionSpec as P


def shifted_2(value, axis, steps):
    count = lax.axis_size(axis)
    first, last = (max(0, -steps), min(count, count - steps))
    return lax.ppermute(value, axis, [(source, source + steps) for source in range(first, last)])


def tap_pieces(extended, top):
    depth = (extended.shape[0] - 1) // 2
    rows = (extended.shape[2] + top - 1) // 2
    cols = extended.shape[3] // 2
    chans = extended.shape[1]
    padded = jnp.pad(extended, ((0, 1), (0, 0), (top, 1), (1, 1)))
    split = padded.reshape(depth + 1, 2, chans, rows + 1, 2, cols + 1, 2)
    pieces = []
    for a in range(3):
        for b in range(3):
            for c in range(3):
                piece = split[
                    a // 2 : a // 2 + depth,
                    a % 2,
                    :,
                    b // 2 : b // 2 + rows,
                    b % 2,
                    c // 2 : c // 2 + cols,
                    c % 2,
                ]
                pieces.append(((a, b, c), piece))
    return pieces


def forward_taps(pieces, kernel):
    total = None
    for (a, b, c), piece in pieces:
        term = jnp.einsum(
            "dkhw,kf->dfhw", piece, kernel[a, b, c], preferred_element_type=jnp.float32
        )
        total = term if total is None else total + term
    return total


def weight_taps(pieces, grad):
    terms = []
    for (a, b, c), piece in pieces:
        terms.append(jnp.einsum("dkhw,dfhw->kf", piece, grad, preferred_element_type=jnp.float32))
    stacked = jnp.stack(terms, 0)
    return stacked.reshape((3, 3, 3) + stacked.shape[1:])


def input_taps(grad_ext, kernel):
    depth = grad_ext.shape[0] - 1
    rows = grad_ext.shape[2] - 1
    cols = grad_ext.shape[3]
    chans = kernel.shape[3]
    parity_taps = ((1,), (2, 0))
    shifted = {}
    for a in range(3):
        for b in range(3):
            for c in range(3):
                term = jnp.einsum(
                    "dfhw,kf->dkhw", grad_ext, kernel[a, b, c], preferred_element_type=jnp.float32
                )
                start_d = 1 if a == 0 else 0
                start_r = 1 if b == 0 else 0
                term = term[start_d : start_d + depth, :, start_r : start_r + rows]
                if c == 0:
                    term = jnp.pad(term[..., 1:], ((0, 0), (0, 0), (0, 0), (0, 1)))
                shifted[a, b, c] = term
    depth_parts = []
    for even_d in range(2):
        row_parts = []
        for even_r in range(2):
            col_parts = []
            for even_c in range(2):
                total = None
                for a in parity_taps[even_d]:
                    for b in parity_taps[even_r]:
                        for c in parity_taps[even_c]:
                            total = shifted[a, b, c] if total is None else total + shifted[a, b, c]
                col_parts.append(total)
            row_parts.append(jnp.stack(col_parts, -1))
        row_parts = jnp.stack(row_parts, 3)
        depth_parts.append(row_parts)
    joined = jnp.stack(depth_parts, 1)
    return joined.reshape(2 * depth, chans, 2 * rows, 2 * cols)


def activation_grad(preact, error):
    sigma = jax.nn.sigmoid(preact)
    return (error * (sigma * (1.0 + preact * (1.0 - sigma)))).astype(jnp.bfloat16)


def on_device(volume, weights, out_error):
    member = lax.axis_index("filt")
    tile = out_error.shape[1]
    below = shifted_2(volume[-1:], "slab", 1)
    extended = jnp.concatenate([below, volume], 0)
    whole = lax.all_gather(extended, "filt", axis=1, tiled=True)
    pieces = tap_pieces(whole, 1)
    kernel_tile = lax.dynamic_slice_in_dim(weights, member * tile, tile, 4)
    preact = forward_taps(pieces, kernel_tile)
    grad = activation_grad(preact, out_error)
    weight_part = weight_taps(pieces, grad)
    grad_rows = lax.all_to_all(grad, "filt", split_axis=2, concat_axis=1, tiled=True)
    count = out_error.shape[0] * lax.axis_size("slab") * out_error.shape[2] * out_error.shape[3]
    weight_grad = lax.psum(weight_part, "slab") * (1.0 / math.sqrt(count))
    upper = shifted_2(grad_rows, "slab", -1)
    grad_ext = jnp.concatenate([grad_rows, upper], 0)
    right_row = shifted_2(grad_ext, "filt", -1)
    grad_ext = jnp.concatenate([grad_ext, right_row], 2)
    in_grad = input_taps(grad_ext, weights).astype(jnp.bfloat16)
    return (in_grad, weight_grad)


def solution(mesh):
    in_specs = (P("slab", "filt", None, None), P(), P("slab", "filt", None, None))
    out_specs = (P("slab", None, "filt", None), P(None, None, None, None, "filt"))
    return jax.shard_map(
        on_device, mesh=mesh, in_specs=in_specs, out_specs=out_specs, check_vma=False
    )
```

profile of v0, /device:TPU:1, one launch (start us, length us, event | category | flops | bytes accessed | tf_op | source)
XLA Modules:
  0.0 422.1 jit_solution(12113445541933201036)
XLA Ops:
  8.1 5.4 %collective-permute-start = (bf16[1,16,16,256]{3,2,1,0:T(8,128)(2,1)S(1)}, bf16[1,16,16,256]{3,2,1,0:T(8,128)(2,1)S(1)}, u32[]{:S(2)}, u32[]{:S(2)}) collective-permute-start(bf16[1,16,16,256]{3,2,1,0:T(8,128)(2,1)S(1)} %slice.347), channel_id=1, source_target_pairs={{0,8},{8,16},{16,24},{24,32},{32,40},{40,48},{48,56},{56,64},{64,7... | collective-permute-start | bytes 393224 | tf_op jit(solution)/shard_map/ppermute | solution.py:11
  13.5 3.6 collective-permute-done
  18.9 51.0 %all-gather.2.cloned.1.call-done = bf16[3,128,16,256]{3,2,1,0:T(8,128)(2,1)} async-done(((bf16[3,16,16,256]{3,2,1,0:T(8,128)(2,1)}), bf16[3,128,16,256]{3,2,1,0:T(8,128)(2,1)}) %all-gather.2.cloned.1.call-update) | async-done | bytes 3145744 | tf_op jit(solution)/shard_map/all_gather | solution.py:104
  69.9 6.1 %copy.203 = bf16[3,128,16,256]{1,0,3,2:T(4,128)(2,1)} copy(bf16[3,128,16,256]{3,2,1,0:T(8,128)(2,1)} %all-gather.2.cloned.1.call-done) | data formatting | bytes 6291456
  76.0 3.9 pad.32.clone
  79.9 4.1 fusion.214
  84.0 11.3 %fusion.213 = (bf16[1,1,128,8,1,128,1]{2,1,0,6,5,4,3:T(2,128)(2,1)}, bf16[1,1,128,8,1,128,1]{2,1,0,6,5,4,3:T(2,128)(2,1)}, bf16[1,1,128,8,1,128,1]{2,1,0,6,5,4,3...) fusion(bf16[2,2,128,9,2,129,2]{2,1,0,6,5,4,3:T(2,128)(2,1)S(1)}, ...), kind=kLoop, calls=%fused_computation.343 | loop fusion | bytes 9961472 | tf_op jit(solution)/shard_map/slice | solution.py:25
  97.4 1.9 copy.158
  101.2 1.9 copy.154
  103.0 1.9 copy.152
  104.9 1.9 copy.150
  106.8 1.9 copy.202
  118.8 1.9 copy.180
  120.7 1.9 copy.178
  122.6 1.9 copy.176
  124.5 1.9 copy.174
  126.3 1.9 copy.172
  128.2 1.9 copy.170
  130.1 1.9 copy.168
  132.0 1.9 copy.166
  165.6 4.6 %all-to-all-start = ((bf16[1,32,8,128]{3,1,0,2:T(8,128)(2,1)}), bf16[1,32,8,128]{3,1,0,2:T(8,128)(2,1)S(1)}, u32[]{:S(2)}, u32[]{:S(2)}) async-start(bf16[1,32,8,128]{3,1,0,2:T(8,128)(2,1)} %bitcast.83), calls=%async_computation | async-start | bytes 131072 | tf_op jit(solution)/shard_map/all_to_all | solution.py:110
  214.3 3.0 collective-permute-start.1
  217.3 3.2 collective-permute-done.1
  221.8 183.9 %all-reduce.12.cloned.1.call-done = f32[3,3,3,128,32]{3,4,2,1,0:T(8,128)} async-done(((f32[3,3,3,128,32]{3,4,2,1,0:T(8,128)}), f32[3,3,3,128,32]{3,4,2,1,0:T(8,128)}) %all-reduce.12.cloned.1.call-update) | async-done | bytes 442384 | tf_op jit(solution)/shard_map/psum | solution.py:112
  (175 shorter events, 102.6 us)
Async XLA Ops:
  7.2 62.7 %all-gather.2.cloned.1.call-start = ((), (), s32[]{:S(2)}) async-start(), calls=%async_computation.1 | async-start | bytes 3538944 | tf_op jit(solution)/shard_map/all_gather | solution.py:104
  8.1 9.0 %collective-permute-start = (bf16[1,16,16,256]{3,2,1,0:T(8,128)(2,1)S(1)}, bf16[1,16,16,256]{3,2,1,0:T(8,128)(2,1)S(1)}, u32[]{:S(2)}, u32[]{:S(2)}) collective-permute-start(bf16[1,16,16,256]{3,2,1,0:T(8,128)(2,1)S(1)} %slice.347), channel_id=1, source_target_pairs={{0,8},{8,16},{16,24},{24,32},{32,40},{40,48},{48,56},{56,64},{64,7... | collective-permute-start | bytes 393224 | tf_op jit(solution)/shard_map/ppermute | solution.py:11
  136.4 7.0 %copy-start.16 = (bf16[1,1,128,8,1,128,1]{5,2,3,6,4,1,0:T(8,128)(2,1)S(1)}, bf16[1,1,128,8,1,128,1]{5,2,3,6,4,1,0:T(8,128)(2,1)}, u32[]{:S(2)}) copy-start(bf16[1,1,128,8,1,128,1]{5,2,3,6,4,1,0:T(8,128)(2,1)} %copy.166) | copy-start | bytes 786436
  137.7 6.8 %copy-start.14 = (bf16[1,1,128,8,1,128,1]{5,2,3,6,4,1,0:T(8,128)(2,1)S(1)}, bf16[1,1,128,8,1,128,1]{5,2,3,6,4,1,0:T(8,128)(2,1)}, u32[]{:S(2)}) copy-start(bf16[1,1,128,8,1,128,1]{5,2,3,6,4,1,0:T(8,128)(2,1)} %copy.168) | copy-start | bytes 786436
  139.0 6.5 %copy-start.11 = (bf16[1,1,128,8,1,128,1]{5,2,3,6,4,1,0:T(8,128)(2,1)S(1)}, bf16[1,1,128,8,1,128,1]{5,2,3,6,4,1,0:T(8,128)(2,1)}, u32[]{:S(2)}) copy-start(bf16[1,1,128,8,1,128,1]{5,2,3,6,4,1,0:T(8,128)(2,1)} %copy.170) | copy-start | bytes 786436
  140.1 6.5 %copy-start.9 = (bf16[1,1,128,8,1,128,1]{5,2,3,6,4,1,0:T(8,128)(2,1)S(1)}, bf16[1,1,128,8,1,128,1]{5,2,3,6,4,1,0:T(8,128)(2,1)}, u32[]{:S(2)}) copy-start(bf16[1,1,128,8,1,128,1]{5,2,3,6,4,1,0:T(8,128)(2,1)} %copy.172) | copy-start | bytes 786436
  141.1 6.5 %copy-start.7 = (bf16[1,1,128,8,1,128,1]{5,2,3,6,4,1,0:T(8,128)(2,1)S(1)}, bf16[1,1,128,8,1,128,1]{5,2,3,6,4,1,0:T(8,128)(2,1)}, u32[]{:S(2)}) copy-start(bf16[1,1,128,8,1,128,1]{5,2,3,6,4,1,0:T(8,128)(2,1)} %copy.174) | copy-start | bytes 786436
  142.2 6.4 %copy-start.5 = (bf16[1,1,128,8,1,128,1]{5,2,3,6,4,1,0:T(8,128)(2,1)S(1)}, bf16[1,1,128,8,1,128,1]{5,2,3,6,4,1,0:T(8,128)(2,1)}, u32[]{:S(2)}) copy-start(bf16[1,1,128,8,1,128,1]{5,2,3,6,4,1,0:T(8,128)(2,1)} %copy.176) | copy-start | bytes 786436
  143.3 6.4 %copy-start.3 = (bf16[1,1,128,8,1,128,1]{5,2,3,6,4,1,0:T(8,128)(2,1)S(1)}, bf16[1,1,128,8,1,128,1]{5,2,3,6,4,1,0:T(8,128)(2,1)}, u32[]{:S(2)}) copy-start(bf16[1,1,128,8,1,128,1]{5,2,3,6,4,1,0:T(8,128)(2,1)} %copy.178) | copy-start | bytes 786436
  157.0 7.0 %copy-start.13 = (bf16[1,1,128,8,1,128,1]{5,2,3,6,4,1,0:T(8,128)(2,1)S(1)}, bf16[1,1,128,8,1,128,1]{5,2,3,6,4,1,0:T(8,128)(2,1)}, u32[]{:S(2)}) copy-start(bf16[1,1,128,8,1,128,1]{5,2,3,6,4,1,0:T(8,128)(2,1)} %copy.150) | copy-start | bytes 786436
  165.6 48.6 %all-to-all-start = ((bf16[1,32,8,128]{3,1,0,2:T(8,128)(2,1)}), bf16[1,32,8,128]{3,1,0,2:T(8,128)(2,1)S(1)}, u32[]{:S(2)}, u32[]{:S(2)}) async-start(bf16[1,32,8,128]{3,1,0,2:T(8,128)(2,1)} %bitcast.83), calls=%async_computation | async-start | bytes 131072 | tf_op jit(solution)/shard_map/all_to_all | solution.py:110
  170.3 235.4 %all-reduce.12.cloned.1.call-start = ((), (), s32[]{:S(2)}) async-start(), calls=%async_computation.2 | async-start | bytes 884736 | tf_op jit(solution)/shard_map/psum | solution.py:112
  170.5 12.3 %copy-start.17 = (bf16[1,1,128,8,1,128,1]{5,2,3,6,4,1,0:T(8,128)(2,1)S(1)}, bf16[1,1,128,8,1,128,1]{5,2,3,6,4,1,0:T(8,128)(2,1)}, u32[]{:S(2)}) copy-start(bf16[1,1,128,8,1,128,1]{5,2,3,6,4,1,0:T(8,128)(2,1)} %copy.166) | copy-start | bytes 786436
  170.5 13.9 %copy-start.15 = (bf16[1,1,128,8,1,128,1]{5,2,3,6,4,1,0:T(8,128)(2,1)S(1)}, bf16[1,1,128,8,1,128,1]{5,2,3,6,4,1,0:T(8,128)(2,1)}, u32[]{:S(2)}) copy-start(bf16[1,1,128,8,1,128,1]{5,2,3,6,4,1,0:T(8,128)(2,1)} %copy.168) | copy-start | bytes 786436
  170.5 15.5 %copy-start.12 = (bf16[1,1,128,8,1,128,1]{5,2,3,6,4,1,0:T(8,128)(2,1)S(1)}, bf16[1,1,128,8,1,128,1]{5,2,3,6,4,1,0:T(8,128)(2,1)}, u32[]{:S(2)}) copy-start(bf16[1,1,128,8,1,128,1]{5,2,3,6,4,1,0:T(8,128)(2,1)} %copy.170) | copy-start | bytes 786436
  170.5 17.2 %copy-start.10 = (bf16[1,1,128,8,1,128,1]{5,2,3,6,4,1,0:T(8,128)(2,1)S(1)}, bf16[1,1,128,8,1,128,1]{5,2,3,6,4,1,0:T(8,128)(2,1)}, u32[]{:S(2)}) copy-start(bf16[1,1,128,8,1,128,1]{5,2,3,6,4,1,0:T(8,128)(2,1)} %copy.172) | copy-start | bytes 786436
  172.4 17.0 %copy-start.8 = (bf16[1,1,128,8,1,128,1]{5,2,3,6,4,1,0:T(8,128)(2,1)S(1)}, bf16[1,1,128,8,1,128,1]{5,2,3,6,4,1,0:T(8,128)(2,1)}, u32[]{:S(2)}) copy-start(bf16[1,1,128,8,1,128,1]{5,2,3,6,4,1,0:T(8,128)(2,1)} %copy.174) | copy-start | bytes 786436
  174.2 16.8 %copy-start.6 = (bf16[1,1,128,8,1,128,1]{5,2,3,6,4,1,0:T(8,128)(2,1)S(1)}, bf16[1,1,128,8,1,128,1]{5,2,3,6,4,1,0:T(8,128)(2,1)}, u32[]{:S(2)}) copy-start(bf16[1,1,128,8,1,128,1]{5,2,3,6,4,1,0:T(8,128)(2,1)} %copy.176) | copy-start | bytes 786436
  176.0 16.7 %copy-start.4 = (bf16[1,1,128,8,1,128,1]{5,2,3,6,4,1,0:T(8,128)(2,1)S(1)}, bf16[1,1,128,8,1,128,1]{5,2,3,6,4,1,0:T(8,128)(2,1)}, u32[]{:S(2)}) copy-start(bf16[1,1,128,8,1,128,1]{5,2,3,6,4,1,0:T(8,128)(2,1)} %copy.178) | copy-start | bytes 786436
  177.8 16.5 %copy-start.2 = (bf16[1,1,128,8,1,128,1]{5,2,3,6,4,1,0:T(8,128)(2,1)S(1)}, bf16[1,1,128,8,1,128,1]{5,2,3,6,4,1,0:T(8,128)(2,1)}, u32[]{:S(2)}) copy-start(bf16[1,1,128,8,1,128,1]{5,2,3,6,4,1,0:T(8,128)(2,1)} %copy.180) | copy-start | bytes 786436
  195.9 16.6 %copy-start.19 = (bf16[1,1,128,8,1,128,1]{5,2,3,6,4,1,0:T(8,128)(2,1)S(1)}, bf16[1,1,128,8,1,128,1]{5,2,3,6,4,1,0:T(8,128)(2,1)}, u32[]{:S(2)}) copy-start(bf16[1,1,128,8,1,128,1]{5,2,3,6,4,1,0:T(8,128)(2,1)} %copy.202) | copy-start | bytes 786436
  207.5 200.0 %copy-start.20 = (bf16[3,3,3,128,256]{4,3,2,1,0:T(8,128)(2,1)S(1)}, bf16[3,3,3,128,256]{4,3,2,1,0:T(8,128)(2,1)}, u32[]{:S(2)}) copy-start(bf16[3,3,3,128,256]{4,3,2,1,0:T(8,128)(2,1)} %param.4) | copy-start | bytes 5308420
  214.3 6.1 %collective-permute-start.1 = (bf16[1,256,1,128]{1,3,2,0:T(8,128)(2,1)S(1)}, bf16[1,256,1,128]{1,3,2,0:T(8,128)(2,1)S(1)}, u32[]{:S(2)}, u32[]{:S(2)}) collective-permute-start(bf16[1,256,1,128]{1,3,2,0:T(8,128)(2,1)S(1)} %copy.115), channel_id=1, source_target_pairs={{8,0},{16,8},{24,16},{32,24},{40,32},{48,40},{56,48},{64,56},{72,6... | collective-permute-start | bytes 196616 | tf_op jit(solution)/shard_map/ppermute | solution.py:11
  220.5 187.0 %collective-permute-start.2 = (bf16[2,256,1,128]{1,3,2,0:T(8,128)(2,1)S(1)}, bf16[2,256,1,128]{1,3,2,0:T(8,128)(2,1)S(1)}, u32[]{:S(2)}, u32[]{:S(2)}) collective-permute-start(bf16[2,256,1,128]{1,3,2,0:T(8,128)(2,1)S(1)} %pad_maximum_fusion.2), channel_id=1, source_target_pairs={{1,0},{2,1},{3,2},{4,3},{5,4},{6,5},{7,6},{9,8},{10,9},{11,10},{12... | collective-permute-start | bytes 393224 | tf_op jit(solution)/shard_map/ppermute | solution.py:11
  (4 other events, 24.1 us)
Sparse Core Ops, SparseCore 0:
  19.0 50.8 all-gather.1
  214.3 191.2 all-reduce.11
where the time goes:
time: 425 us; the launch traced here: 422 us
  waiting for transfers between devices  242 us (57%)
  matrix products  80.7 us (19%)
  local copies, waits for them, and re-layouts  66.4 us (16%)
  between operations  15 us (4%)
  starting transfers between devices  14.5 us (3%)
    psum x1, waiting for transfers between devices, on_device(): weight_grad = lax.psum(weight_part, 'slab') * (1.0 / math.sqrt(count))  184 us
    all_gather x1, waiting for transfers between devices, on_device(): whole = lax.all_gather(extended, 'filt', axis=1, tiled=True)  51 us
    unnamed x73, local copies, waits for them, and re-layouts  45.6 us
    dot_general x27, matrix products, weight_taps(): jnp.einsum('dkhw,dfhw->kf', piece, grad, preferred_element_type=jnp.float32)  45.2 us
    dot_general x27, matrix products, forward_taps(): jnp.einsum('dkhw,kf->dfhw', piece, kernel[a, b, c], preferred_element_typ...  29.6 us
    slice x2, local copies, waits for them, and re-layouts, tap_pieces(): split[a // 2:a // 2 + depth, a % 2, :, b // 2:b // 2 + rows, b % 2, c //...  15.4 us
    ppermute x3, starting transfers between devices, shifted_2(): lax.ppermute(value, axis, [(source, source + steps) for source in range(f...  9.64 us
  transfers between devices with their start and end apart: 6, of which 4 were waited for; matrix products, arithmetic and copies ran while one was open for 11% of the time, Pallas kernels for 0%

commit v1 on v0

--- a/solution.py
+++ b/solution.py
@@ -101,7 +101,19 @@
     tile = out_error.shape[1]
     below = shifted_2(volume[-1:], "slab", 1)
     extended = jnp.concatenate([below, volume], 0)
-    whole = lax.all_gather(extended, "filt", axis=1, tiled=True)
+
+    def _handle_tails(xs, dev_axis):
+        return jnp.concatenate(
+            lax.all_to_all(
+                jnp.stack(lax.axis_size(dev_axis) * [xs]),
+                axis_name=dev_axis,
+                split_axis=0,
+                concat_axis=0,
+            ),
+            axis=1,
+        )
+
+    whole = _handle_tails(extended, "filt")
     pieces = tap_pieces(whole, 1)
     kernel_tile = lax.dynamic_slice_in_dim(weights, member * tile, tile, 4)
     preact = forward_taps(pieces, kernel_tile)

time: 425 us -> 456 us (1.073)
  waiting for transfers between devices: 242 us -> 267 us
    all_to_all x0 -> x1, waiting for transfers between devices: none -> 74.2 us  [_handle_tails(): lax.all_to_all(jnp.stack(lax.axis_size(dev_axis) * [xs]), axis_name=dev_a...]
    all_gather x1 -> x0, waiting for transfers between devices: 51 us -> none  [on_device(): whole = lax.all_gather(extended, 'filt', axis=1, tiled=True)]
    all_to_all x0 -> x1, starting transfers between devices: none -> 5.15 us  [_handle_tails(): lax.all_to_all(jnp.stack(lax.axis_size(dev_axis) * [xs]), axis_name=dev_a...]
  transfers between devices with their start and end apart: 6 -> 6, of which waited for: 4 -> 4; matrix products, arithmetic and copies ran while one was open for 11% -> 10% of each run, Pallas kernels for 0% -> 0%
where the time goes in v1:
time: 456 us; the launch traced here: 452 us
  waiting for transfers between devices  267 us (59%)
  matrix products  80.7 us (18%)
  local copies, waits for them, and re-layouts  68.8 us (15%)
  starting transfers between devices  17.7 us (4%)
  between operations  15 us (3%)
    psum x1, waiting for transfers between devices, on_device(): weight_grad = lax.psum(weight_part, 'slab') * (1.0 / math.sqrt(count))  185 us
    all_to_all x1, waiting for transfers between devices, _handle_tails(): lax.all_to_all(jnp.stack(lax.axis_size(dev_axis) * [xs]), axis_name=dev_a...  74.2 us
    dot_general x27, matrix products, weight_taps(): jnp.einsum('dkhw,dfhw->kf', piece, grad, preferred_element_type=jnp.float32)  45.2 us
    unnamed x73, local copies, waits for them, and re-layouts  43.9 us
    dot_general x27, matrix products, forward_taps(): jnp.einsum('dkhw,kf->dfhw', piece, kernel[a, b, c], preferred_element_typ...  29.6 us
    slice x2, local copies, waits for them, and re-layouts, tap_pieces(): split[a // 2:a // 2 + depth, a % 2, :, b // 2:b // 2 + rows, b % 2, c //...  15.4 us
  transfers between devices with their start and end apart: 6, of which 4 were waited for; matrix products, arithmetic and copies ran while one was open for 10% of the time, Pallas kernels for 0%

profile of v1, /device:TPU:1, one launch (start us, length us, event | category | flops | bytes accessed | tf_op | source)
XLA Modules:
  0.0 452.5 jit_solution(12254983364456366161)
XLA Ops:
  8.1 5.4 %collective-permute-start = (bf16[1,16,16,256]{3,2,1,0:T(8,128)(2,1)S(1)}, bf16[1,16,16,256]{3,2,1,0:T(8,128)(2,1)S(1)}, u32[]{:S(2)}, u32[]{:S(2)}) collective-permute-start(bf16[1,16,16,256]{3,2,1,0:T(8,128)(2,1)S(1)} %slice.347), channel_id=1, source_target_pairs={{0,8},{8,16},{16,24},{24,32},{32,40},{40,48},{48,56},{56,64},{64,7... | collective-permute-start | bytes 393224 | tf_op jit(solution)/shard_map/ppermute | solution.py:11
  13.5 3.6 collective-permute-done
  18.1 2.0 stack.166
  20.1 5.1 %all-to-all-start = ((bf16[8,3,16,16,256]{4,3,2,1,0:T(8,128)(2,1)}), bf16[8,3,16,16,256]{4,3,2,1,0:T(8,128)(2,1)}, u32[]{:S(2)}, u32[]{:S(2)}) async-start(bf16[8,3,16,16,256]{4,3,2,1,0:T(8,128)(2,1)} %stack.166), calls=%async_computation | async-start | bytes 6291456 | tf_op jit(solution)/shard_map/all_to_all | solution.py:107
  25.3 74.2 %all-to-all-done = bf16[8,3,16,16,256]{4,3,2,1,0:T(8,128)(2,1)} async-done(((bf16[8,3,16,16,256]{4,3,2,1,0:T(8,128)(2,1)}), bf16[8,3,16,16,256]{4,3,2,1,0:T(8,128)(2,1)}, u32[]{:S(2)}, u32[]{:S(2)}) %all-to-all-start) | async-done | bytes 3145760 | tf_op jit(solution)/shard_map/all_to_all | solution.py:107
  99.5 2.2 copy.86
  101.7 4.3 copy.205
  106.0 3.9 pad.32.clone
  109.9 4.1 fusion.214
  114.0 11.3 %fusion.213 = (bf16[1,1,128,8,1,128,1]{2,1,0,6,5,4,3:T(2,128)(2,1)}, bf16[1,1,128,8,1,128,1]{2,1,0,6,5,4,3:T(2,128)(2,1)}, bf16[1,1,128,8,1,128,1]{2,1,0,6,5,4,3...) fusion(bf16[2,2,128,9,2,129,2]{2,1,0,6,5,4,3:T(2,128)(2,1)S(1)}, ...), kind=kLoop, calls=%fused_computation.343 | loop fusion | bytes 9961472 | tf_op jit(solution)/shard_map/slice | solution.py:25
  127.4 1.9 copy.160
  129.3 1.9 copy.158
  133.0 1.9 copy.154
  134.9 1.9 copy.152
  136.8 1.9 copy.204
  148.8 1.9 copy.182
  156.3 1.9 copy.174
  158.2 1.9 copy.172
  160.1 1.9 copy.170
  162.0 1.9 copy.168
  195.7 3.5 all-to-all-start.1
  243.1 2.3 collective-permute-start.1
  245.4 4.1 collective-permute-done.1
  250.8 185.2 %all-reduce.12.cloned.1.call-done = f32[3,3,3,128,32]{3,4,2,1,0:T(8,128)} async-done(((f32[3,3,3,128,32]{3,4,2,1,0:T(8,128)}), f32[3,3,3,128,32]{3,4,2,1,0:T(8,128)}) %all-reduce.12.cloned.1.call-update) | async-done | bytes 442384 | tf_op jit(solution)/shard_map/psum | solution.py:124
  (176 shorter events, 107.3 us)
Async XLA Ops:
  8.1 9.0 %collective-permute-start = (bf16[1,16,16,256]{3,2,1,0:T(8,128)(2,1)S(1)}, bf16[1,16,16,256]{3,2,1,0:T(8,128)(2,1)S(1)}, u32[]{:S(2)}, u32[]{:S(2)}) collective-permute-start(bf16[1,16,16,256]{3,2,1,0:T(8,128)(2,1)S(1)} %slice.347), channel_id=1, source_target_pairs={{0,8},{8,16},{16,24},{24,32},{32,40},{40,48},{48,56},{56,64},{64,7... | collective-permute-start | bytes 393224 | tf_op jit(solution)/shard_map/ppermute | solution.py:11
  20.1 79.4 %all-to-all-start = ((bf16[8,3,16,16,256]{4,3,2,1,0:T(8,128)(2,1)}), bf16[8,3,16,16,256]{4,3,2,1,0:T(8,128)(2,1)}, u32[]{:S(2)}, u32[]{:S(2)}) async-start(bf16[8,3,16,16,256]{4,3,2,1,0:T(8,128)(2,1)} %stack.166), calls=%async_computation | async-start | bytes 6291456 | tf_op jit(solution)/shard_map/all_to_all | solution.py:107
  166.4 7.0 %copy-start.16 = (bf16[1,1,128,8,1,128,1]{5,2,3,6,4,1,0:T(8,128)(2,1)S(1)}, bf16[1,1,128,8,1,128,1]{5,2,3,6,4,1,0:T(8,128)(2,1)}, u32[]{:S(2)}) copy-start(bf16[1,1,128,8,1,128,1]{5,2,3,6,4,1,0:T(8,128)(2,1)} %copy.168) | copy-start | bytes 786436
  167.7 6.8 %copy-start.14 = (bf16[1,1,128,8,1,128,1]{5,2,3,6,4,1,0:T(8,128)(2,1)S(1)}, bf16[1,1,128,8,1,128,1]{5,2,3,6,4,1,0:T(8,128)(2,1)}, u32[]{:S(2)}) copy-start(bf16[1,1,128,8,1,128,1]{5,2,3,6,4,1,0:T(8,128)(2,1)} %copy.170) | copy-start | bytes 786436
  169.0 6.5 %copy-start.11 = (bf16[1,1,128,8,1,128,1]{5,2,3,6,4,1,0:T(8,128)(2,1)S(1)}, bf16[1,1,128,8,1,128,1]{5,2,3,6,4,1,0:T(8,128)(2,1)}, u32[]{:S(2)}) copy-start(bf16[1,1,128,8,1,128,1]{5,2,3,6,4,1,0:T(8,128)(2,1)} %copy.172) | copy-start | bytes 786436
  170.1 6.5 %copy-start.9 = (bf16[1,1,128,8,1,128,1]{5,2,3,6,4,1,0:T(8,128)(2,1)S(1)}, bf16[1,1,128,8,1,128,1]{5,2,3,6,4,1,0:T(8,128)(2,1)}, u32[]{:S(2)}) copy-start(bf16[1,1,128,8,1,128,1]{5,2,3,6,4,1,0:T(8,128)(2,1)} %copy.174) | copy-start | bytes 786436
  171.2 6.5 %copy-start.7 = (bf16[1,1,128,8,1,128,1]{5,2,3,6,4,1,0:T(8,128)(2,1)S(1)}, bf16[1,1,128,8,1,128,1]{5,2,3,6,4,1,0:T(8,128)(2,1)}, u32[]{:S(2)}) copy-start(bf16[1,1,128,8,1,128,1]{5,2,3,6,4,1,0:T(8,128)(2,1)} %copy.176) | copy-start | bytes 786436
  172.3 6.4 %copy-start.5 = (bf16[1,1,128,8,1,128,1]{5,2,3,6,4,1,0:T(8,128)(2,1)S(1)}, bf16[1,1,128,8,1,128,1]{5,2,3,6,4,1,0:T(8,128)(2,1)}, u32[]{:S(2)}) copy-start(bf16[1,1,128,8,1,128,1]{5,2,3,6,4,1,0:T(8,128)(2,1)} %copy.178) | copy-start | bytes 786436
  173.4 6.4 %copy-start.3 = (bf16[1,1,128,8,1,128,1]{5,2,3,6,4,1,0:T(8,128)(2,1)S(1)}, bf16[1,1,128,8,1,128,1]{5,2,3,6,4,1,0:T(8,128)(2,1)}, u32[]{:S(2)}) copy-start(bf16[1,1,128,8,1,128,1]{5,2,3,6,4,1,0:T(8,128)(2,1)} %copy.180) | copy-start | bytes 786436
  187.1 7.0 %copy-start.13 = (bf16[1,1,128,8,1,128,1]{5,2,3,6,4,1,0:T(8,128)(2,1)S(1)}, bf16[1,1,128,8,1,128,1]{5,2,3,6,4,1,0:T(8,128)(2,1)}, u32[]{:S(2)}) copy-start(bf16[1,1,128,8,1,128,1]{5,2,3,6,4,1,0:T(8,128)(2,1)} %copy.152) | copy-start | bytes 786436
  195.7 47.3 %all-to-all-start.1 = ((bf16[1,32,8,128]{3,1,0,2:T(8,128)(2,1)}), bf16[1,32,8,128]{3,1,0,2:T(8,128)(2,1)S(1)}, u32[]{:S(2)}, u32[]{:S(2)}) async-start(bf16[1,32,8,128]{3,1,0,2:T(8,128)(2,1)} %bitcast.85), calls=%async_computation.1 | async-start | bytes 131072 | tf_op jit(solution)/shard_map/all_to_all | solution.py:122
  199.2 236.8 %all-reduce.12.cloned.1.call-start = ((), (), s32[]{:S(2)}) async-start(), calls=%async_computation.2 | async-start | bytes 884736 | tf_op jit(solution)/shard_map/psum | solution.py:124
  199.2 12.3 %copy-start.17 = (bf16[1,1,128,8,1,128,1]{5,2,3,6,4,1,0:T(8,128)(2,1)S(1)}, bf16[1,1,128,8,1,128,1]{5,2,3,6,4,1,0:T(8,128)(2,1)}, u32[]{:S(2)}) copy-start(bf16[1,1,128,8,1,128,1]{5,2,3,6,4,1,0:T(8,128)(2,1)} %copy.168) | copy-start | bytes 786436
  199.3 13.9 %copy-start.15 = (bf16[1,1,128,8,1,128,1]{5,2,3,6,4,1,0:T(8,128)(2,1)S(1)}, bf16[1,1,128,8,1,128,1]{5,2,3,6,4,1,0:T(8,128)(2,1)}, u32[]{:S(2)}) copy-start(bf16[1,1,128,8,1,128,1]{5,2,3,6,4,1,0:T(8,128)(2,1)} %copy.170) | copy-start | bytes 786436
  199.3 15.5 %copy-start.12 = (bf16[1,1,128,8,1,128,1]{5,2,3,6,4,1,0:T(8,128)(2,1)S(1)}, bf16[1,1,128,8,1,128,1]{5,2,3,6,4,1,0:T(8,128)(2,1)}, u32[]{:S(2)}) copy-start(bf16[1,1,128,8,1,128,1]{5,2,3,6,4,1,0:T(8,128)(2,1)} %copy.172) | copy-start | bytes 786436
  199.3 17.2 %copy-start.10 = (bf16[1,1,128,8,1,128,1]{5,2,3,6,4,1,0:T(8,128)(2,1)S(1)}, bf16[1,1,128,8,1,128,1]{5,2,3,6,4,1,0:T(8,128)(2,1)}, u32[]{:S(2)}) copy-start(bf16[1,1,128,8,1,128,1]{5,2,3,6,4,1,0:T(8,128)(2,1)} %copy.174) | copy-start | bytes 786436
  201.1 17.0 %copy-start.8 = (bf16[1,1,128,8,1,128,1]{5,2,3,6,4,1,0:T(8,128)(2,1)S(1)}, bf16[1,1,128,8,1,128,1]{5,2,3,6,4,1,0:T(8,128)(2,1)}, u32[]{:S(2)}) copy-start(bf16[1,1,128,8,1,128,1]{5,2,3,6,4,1,0:T(8,128)(2,1)} %copy.176) | copy-start | bytes 786436
  202.9 16.8 %copy-start.6 = (bf16[1,1,128,8,1,128,1]{5,2,3,6,4,1,0:T(8,128)(2,1)S(1)}, bf16[1,1,128,8,1,128,1]{5,2,3,6,4,1,0:T(8,128)(2,1)}, u32[]{:S(2)}) copy-start(bf16[1,1,128,8,1,128,1]{5,2,3,6,4,1,0:T(8,128)(2,1)} %copy.178) | copy-start | bytes 786436
  204.7 16.7 %copy-start.4 = (bf16[1,1,128,8,1,128,1]{5,2,3,6,4,1,0:T(8,128)(2,1)S(1)}, bf16[1,1,128,8,1,128,1]{5,2,3,6,4,1,0:T(8,128)(2,1)}, u32[]{:S(2)}) copy-start(bf16[1,1,128,8,1,128,1]{5,2,3,6,4,1,0:T(8,128)(2,1)} %copy.180) | copy-start | bytes 786436
  206.5 16.5 %copy-start.2 = (bf16[1,1,128,8,1,128,1]{5,2,3,6,4,1,0:T(8,128)(2,1)S(1)}, bf16[1,1,128,8,1,128,1]{5,2,3,6,4,1,0:T(8,128)(2,1)}, u32[]{:S(2)}) copy-start(bf16[1,1,128,8,1,128,1]{5,2,3,6,4,1,0:T(8,128)(2,1)} %copy.182) | copy-start | bytes 786436
  224.7 16.6 %copy-start.19 = (bf16[1,1,128,8,1,128,1]{5,2,3,6,4,1,0:T(8,128)(2,1)S(1)}, bf16[1,1,128,8,1,128,1]{5,2,3,6,4,1,0:T(8,128)(2,1)}, u32[]{:S(2)}) copy-start(bf16[1,1,128,8,1,128,1]{5,2,3,6,4,1,0:T(8,128)(2,1)} %copy.204) | copy-start | bytes 786436
  236.2 201.6 %copy-start.20 = (bf16[3,3,3,128,256]{4,3,2,1,0:T(8,128)(2,1)S(1)}, bf16[3,3,3,128,256]{4,3,2,1,0:T(8,128)(2,1)}, u32[]{:S(2)}) copy-start(bf16[3,3,3,128,256]{4,3,2,1,0:T(8,128)(2,1)} %param.4) | copy-start | bytes 5308420
  243.1 6.4 %collective-permute-start.1 = (bf16[1,256,1,128]{1,3,2,0:T(8,128)(2,1)S(1)}, bf16[1,256,1,128]{1,3,2,0:T(8,128)(2,1)S(1)}, u32[]{:S(2)}, u32[]{:S(2)}) collective-permute-start(bf16[1,256,1,128]{1,3,2,0:T(8,128)(2,1)S(1)} %copy.117), channel_id=1, source_target_pairs={{8,0},{16,8},{24,16},{32,24},{40,32},{48,40},{56,48},{64,56},{72,6... | collective-permute-start | bytes 196616 | tf_op jit(solution)/shard_map/ppermute | solution.py:11
  249.5 188.3 %collective-permute-start.2 = (bf16[2,256,1,128]{1,3,2,0:T(8,128)(2,1)S(1)}, bf16[2,256,1,128]{1,3,2,0:T(8,128)(2,1)S(1)}, u32[]{:S(2)}, u32[]{:S(2)}) collective-permute-start(bf16[2,256,1,128]{1,3,2,0:T(8,128)(2,1)S(1)} %pad_maximum_fusion.2), channel_id=1, source_target_pairs={{1,0},{2,1},{3,2},{4,3},{5,4},{6,5},{7,6},{9,8},{10,9},{11,10},{12... | collective-permute-start | bytes 393224 | tf_op jit(solution)/shard_map/ppermute | solution.py:11
  (4 other events, 24.1 us)
Sparse Core Ops, SparseCore 0:
  243.1 192.8 all-reduce.11
